TPU v7x, 32 devices: a whole 2x2x4 slice. The times are simulated.
32 devices in a mesh: groups: 2 (over x), blk: 16 (over z, y, core).
Axes of the slice: x: 2, y: 2, z: 4, core: 2. Of those that a mesh axis runs over, the one named last changes fastest.
Arguments:
- queries: bfloat16 [32768, 1024], P(('groups', 'blk')), parts along dimension 0, may hold values from -2.5 to 2.5
- passages: bfloat16 [128, 256, 1024], P('blk', 'groups'), parts along dimension 1, may hold values from -12 to 12
- block_list: int32 [256, 4], P(('groups', 'blk')), parts along dimension 0, may hold values from 0 to 127, as said below
- pair_count: int32 [256], P(('groups', 'blk')), parts along dimension 0, may hold values from 1 to 4, 256 in all
- positive: int32 [32768], P(('groups', 'blk')), parts along dimension 0, may hold values from 0 to 511
Outputs:
- row_loss: float32 [32768], P(('groups', 'blk')), parts along dimension 0
- query_grad: bfloat16 [32768, 1024], P(('groups', 'blk')), parts along dimension 0
- passage_grad: bfloat16 [128, 256, 1024], P('blk', 'groups'), parts along dimension 1
There are 2 independent parts, one for each index of `groups`. A program takes and returns all parts, laid end to end along the dimension named above; each array names one. Nothing has to cross between parts.
Inputs may be any that keep to these rules, and one draw needn't show every extreme that they name: `block_list`: each row names 4 different passage blocks; the 8 rows of one index of blk (aligned runs of 8 rows) name exactly 8 different passage blocks in all, each of them in the same number of rows. `pair_count`: the 128 entries of one group sum to 256, and some entry of each group equals 4; the sum holds for each group separately, not over all groups together.
All inputs are finite; a program needn't handle non-finite values.
Results may differ from a plain program's by a relative error of at most 0.0039.
Values may be sent and summed in bfloat16 or wider, within the bound.
A program may use at most 128 MiB of HBM per device.

v0:
```python
import jax
import jax.numpy as jnp
from jax import lax
from jax.sharding import PartitionSpec as P

D = 1024
BLK = 128
NB = 4
DISTINCT = 8


def send_back(partial_value):
    return lax.all_to_all(partial_value, "blk", split_axis=0, concat_axis=1, tiled=True)


def body(queries, passages, block_list, pair_count, positive):
    qblocks_here = block_list.shape[0]
    listed = block_list.reshape(-1)
    pair_total = listed.shape[0]
    span_cols = NB * BLK
    ordered = jnp.sort(listed)
    fresh = jnp.concatenate([jnp.ones((1,), jnp.bool_), ordered[1:] != ordered[:-1]])
    rank_of = jnp.cumsum(fresh.astype(jnp.int32)) - 1
    wanted = jnp.full((DISTINCT,), -1, jnp.int32).at[rank_of].set(ordered)
    matches = listed[:, None] == wanted[None, :]
    slot_index = jnp.sum(
        matches.astype(jnp.int32) * jnp.arange(DISTINCT, dtype=jnp.int32)[None, :], axis=1
    )
    merge_table = matches.astype(jnp.float32)
    requests = lax.all_gather(jnp.maximum(wanted, 0), "blk", axis=0, tiled=True)
    served = passages[:, requests, :]
    fetched = lax.all_to_all(served, "blk", split_axis=1, concat_axis=0, tiled=True)
    candidates = fetched[:, slot_index, :].reshape(BLK, qblocks_here, NB, D)
    query_rows = queries.reshape(qblocks_here, BLK, D)
    scores = jnp.einsum(
        "grd,cgnd->grnc", query_rows, candidates, preferred_element_type=jnp.float32
    )
    scores = scores.reshape(qblocks_here, BLK, span_cols)
    columns = jnp.arange(span_cols, dtype=jnp.int32)
    live_limit = pair_count * BLK
    is_live = columns[None, None, :] < live_limit[:, None, None]
    target_slot = positive.reshape(qblocks_here, BLK) % live_limit[:, None]
    row_max = jnp.max(jnp.where(is_live, scores, -jnp.inf), axis=2, keepdims=True)
    weights = jnp.where(is_live, jnp.exp(scores - row_max), jnp.float32(0.0))
    row_sum = jnp.sum(weights, axis=2, keepdims=True)
    target = jnp.take_along_axis(scores, target_slot[:, :, None], axis=2)[:, :, 0]
    row_loss = row_max[:, :, 0] + jnp.log(row_sum[:, :, 0]) - target
    onehot = (columns[None, None, :] == target_slot[:, :, None]).astype(jnp.float32)
    grad_scores = (
        (weights / row_sum - onehot).astype(jnp.bfloat16).reshape(qblocks_here, BLK, NB, BLK)
    )
    contrib = jnp.einsum(
        "grnc,grd->cgnd", grad_scores, query_rows, preferred_element_type=jnp.float32
    )
    contrib = contrib.reshape(BLK, pair_total, D)
    partial_value = jnp.einsum("cpd,pk->ckd", contrib, merge_table, precision=lax.Precision.HIGHEST)
    query_grad = jnp.einsum(
        "grnc,cgnd->grd", grad_scores, candidates, preferred_element_type=jnp.float32
    ).astype(jnp.bfloat16)
    returned = send_back(partial_value)
    passage_grad = jnp.zeros(passages.shape, jnp.float32).at[:, requests, :].add(returned)
    return (row_loss.reshape(-1), query_grad.reshape(-1, D), passage_grad.astype(jnp.bfloat16))


def solution(mesh):
    return jax.shard_map(
        body,
        mesh=mesh,
        in_specs=(
            P(("groups", "blk"), None),
            P("blk", "groups", None),
            P(("groups", "blk"), None),
            P(("groups", "blk")),
            P(("groups", "blk")),
        ),
        out_specs=(P(("groups", "blk")), P(("groups", "blk"), None), P("blk", "groups", None)),
        check_vma=False,
    )
```

profile of v0, /device:TPU:15, one launch (start us, length us, event | category | flops | bytes accessed | tf_op | source)
XLA Modules:
  0.0 248.9 jit_solution(7454822869387522437)
XLA Ops:
  0.7 0.9 copy.39
  1.6 1.6 sort.15
  3.7 1.2 dynamic-slice
  6.4 7.9 %all-reduce = s32[128]{0:T(128)S(1)} all-reduce(s32[128]{0:T(128)S(1)} %maximum_dynamic-update-slice_fusion), channel_id=1, replica_groups=mesh['groups'=2,'blk'=16] {'blk'}, use_global_device_ids=true, to_apply=%add | all-reduce | flops 128 | bytes 1024
  14.3 7.5 %gather_fusion = bf16[128,8,1024]{2,0,1:T(8,128)(2,1)} fusion(bf16[8,128,1024]{2,1,0:T(8,128)(2,1)} %param.6, s32[1024]{0:T(1024)S(1)} %pad_clamp_fusion.1), kind=kCustom, calls=%fused_computation | custom fusion | bytes 4194816 | tf_op jit(solution)/shard_map/gather | solution.py:31
  21.8 4.1 %copy.41 = bf16[8,128,1024]{2,0,1:T(8,128)(2,1)} copy(bf16[8,128,1024]{2,1,0:T(8,128)(2,1)} %bitcast.88) | data formatting | bytes 4194304 | tf_op jit(solution)/shard_map/gather | solution.py:31
  25.8 9.4 %all-to-all-start = ((bf16[8,128,1024]{2,0,1:T(8,128)(2,1)}), bf16[8,128,1024]{2,0,1:T(8,128)(2,1)}, u32[]{:S(2)}, u32[]{:S(2)}) async-start(bf16[8,128,1024]{2,0,1:T(8,128)(2,1)} %copy.41), calls=%async_computation | async-start | bytes 4194304 | tf_op jit(solution)/shard_map/all_to_all | solution.py:32
  35.9 46.9 %all-to-all-done = bf16[8,128,1024]{2,0,1:T(8,128)(2,1)} async-done(((bf16[8,128,1024]{2,0,1:T(8,128)(2,1)}), bf16[8,128,1024]{2,0,1:T(8,128)(2,1)}, u32[]{:S(2)}, u32[]{:S(2)}) %all-to-all-start) | async-done | bytes 2097184 | tf_op jit(solution)/shard_map/all_to_all | solution.py:32
  82.8 3.0 %copy.43 = bf16[16,8,8,1024]{3,2,1,0:T(8,128)(2,1)S(1)} copy(bf16[16,8,8,1024]{3,1,2,0:T(8,128)(2,1)} %bitcast.5) | data formatting | bytes 4194304 | tf_op jit(solution)/shard_map/all_to_all | solution.py:32
  85.8 2.5 copy.47
  88.3 6.5 %gather_fusion.1 = bf16[32,128,1024]{2,1,0:T(8,128)(2,1)} fusion(bf16[128,8,1024]{2,0,1:T(8,128)(2,1)} %copy.47, s32[1024]{0:T(1024)S(1)} %pad_clamp_fusion), kind=kCustom, calls=%fused_computation.1 | custom fusion | bytes 16777344 | tf_op jit(solution)/shard_map/gather | solution.py:33
  94.8 4.8 %fusion.5 = (f32[8,128]{1,0:T(8,128)S(1)}, f32[8,128,4,128]{3,1,2,0:T(8,128)S(1)}) fusion(pred[8,4,128]{2,1,0:T(4,128)(4,1)S(1)} %broadcast_compare_fusion, bf16[128,8,4,1024]{3,0,2,1:T(8,128)(2,1)} %bitcast.85, bf16[8,128,1024,1]{2,1,3,0:T(8,128)(2,1)S(1)} %bitcast.80), kind=kOutput, calls=%fused_computation.11 | convolution fusion | flops 1074789376 | bytes 12591104 | tf_op jit(solution)/shard_map/grd,cgnd->grnc/dot_general | solution.py:35
  100.3 2.5 fusion.23
  102.8 13.3 %fusion.2 = f32[128,8,1024]{2,1,0:T(8,128)} fusion(f32[128,32,1024]{2,0,1:T(8,128)S(1)} %bitcast.82, s32[32]{0:T(128)S(1)} %reshape.340, s32[8]{0:T(128)S(1)} %scatter_custom_fusion), kind=kOutput, calls=%fused_computation.8 | convolution fusion | flops 402653440 | bytes 20971680 | tf_op jit(solution)/shard_map/cpd,pk->ckd/dot_general | solution.py:56
  116.1 4.9 %all-to-all-start.1 = ((f32[128,8,1024]{2,1,0:T(8,128)}), f32[128,8,1024]{2,1,0:T(8,128)}, u32[]{:S(2)}, u32[]{:S(2)}) async-start(f32[128,8,1024]{2,1,0:T(8,128)} %fusion.2), calls=%async_computation.1 | async-start | bytes 8388608 | tf_op jit(solution)/shard_map/all_to_all | solution.py:13
  121.3 14.8 %gather_fusion.2 = f32[1024]{0:T(1024)S(1)} fusion(f32[8,128,512]{1,2,0:T(8,128)} %bitcast.83, s32[1024]{0:T(1024)S(1)} %fusion.14), kind=kCustom, calls=%fused_computation.2 | custom fusion | bytes 20480 | tf_op jit(solution)/shard_map/jit(take_along_axis)/gather | solution.py:46
  136.1 0.7 bitcast_subtract_fusion.1
  136.8 7.3 %bitcast_convert_fusion = bf16[8,128,1024]{2,1,0:T(8,128)(2,1)} fusion(bf16[128,8,4,1024]{3,0,2,1:T(8,128)(2,1)} %bitcast.86, f32[8,128,4,128]{3,1,2,0:T(8,128)} %copy-done.1, s32[8,128]{1,0:T(8,128)S(1)} %add_select_fusion, s32[4,128]{1,0:T(4,128)S(1)} %multiply_add_fusion, f32[8,128]{1,0:T(8,128)S(1)} %fusion.8, f32[8,128]{1,0:T(8,128)S(1)} %get-tuple-element.20, ...), kind=kOutput, calls=%fused_computation.7 | convolution fusion | flops 1078460416 | bytes 12601344 | tf_op jit(solution)/shard_map/grnc,cgnd->grd/dot_general | solution.py:57
  144.2 69.3 %all-to-all-done.1 = f32[128,8,1024]{2,1,0:T(8,128)} async-done(((f32[128,8,1024]{2,1,0:T(8,128)}), f32[128,8,1024]{2,1,0:T(8,128)}, u32[]{:S(2)}, u32[]{:S(2)}) %all-to-all-start.1) | async-done | bytes 4194336 | tf_op jit(solution)/shard_map/all_to_all | solution.py:13
  213.5 7.7 %copy.50 = f32[8,16,8,1024]{3,0,2,1:T(8,128)} copy(f32[8,16,8,1024]{3,2,0,1:T(8,128)} %bitcast.33) | data formatting | bytes 8388608 | tf_op jit(solution)/shard_map/all_to_all | solution.py:13
  221.2 2.5 %broadcast_in_dim.50 = f32[8,128,1024]{2,0,1:T(8,128)} broadcast(f32[]{:T(128)} %constant.47.clone.1), dimensions={} | broadcast | bytes 4194308 | tf_op jit(solution)/shard_map/broadcast_in_dim | solution.py:61
  223.7 20.2 %scatter_fusion = f32[8,128,1024]{2,0,1:T(8,128)} fusion(f32[8,128,1024]{2,0,1:T(8,128)} %broadcast_in_dim.50, s32[128]{0:T(128)S(1)} %compare_select_fusion.6, f32[128,8,1024]{2,1,0:T(8,128)} %bitcast.84), kind=kCustom, calls=%fused_computation.4 | custom fusion | flops 1048576 | bytes 12583424 | tf_op jit(solution)/shard_map/scatter-add | solution.py:61
  243.9 2.5 %convert_element_type.30 = bf16[8,128,1024]{2,0,1:T(8,128)(2,1)S(1)} convert(f32[8,128,1024]{2,0,1:T(8,128)} %scatter_fusion) | non-fusion elementwise | flops 1048576 | bytes 6291456 | tf_op jit(solution)/shard_map/convert_element_type | solution.py:62
  246.4 2.5 copy.51
  (36 shorter events, 2.9 us)
Async XLA Ops:
  0.6 94.2 %copy-start = (bf16[1024,1024]{1,0:T(8,128)(2,1)S(1)}, bf16[1024,1024]{1,0:T(8,128)(2,1)}, u32[]{:S(2)}) copy-start(bf16[1024,1024]{1,0:T(8,128)(2,1)} %param.5) | copy-start | bytes 6291460
  25.8 9.7 %copy-start.3 = (s32[8]{0:T(128)S(1)}, s32[8]{0:T(128)}, u32[]{:S(2)}) copy-start(s32[8]{0:T(128)} %param.8) | copy-start | bytes 100
  25.8 9.8 %copy-start.2 = (s32[1024]{0:T(1024)S(1)}, s32[1024]{0:T(1024)}, u32[]{:S(2)}) copy-start(s32[1024]{0:T(1024)} %param.9) | copy-start | bytes 12292
  25.8 57.0 %all-to-all-start = ((bf16[8,128,1024]{2,0,1:T(8,128)(2,1)}), bf16[8,128,1024]{2,0,1:T(8,128)(2,1)}, u32[]{:S(2)}, u32[]{:S(2)}) async-start(bf16[8,128,1024]{2,0,1:T(8,128)(2,1)} %copy.41), calls=%async_computation | async-start | bytes 4194304 | tf_op jit(solution)/shard_map/all_to_all | solution.py:32
  99.6 3.2 %copy-start.1 = (f32[8,128,4,128]{3,1,2,0:T(8,128)}, f32[8,128,4,128]{3,1,2,0:T(8,128)S(1)}, u32[]{:S(2)}) copy-start(f32[8,128,4,128]{3,1,2,0:T(8,128)S(1)} %get-tuple-element.21) | copy-start | bytes 6291460
  116.1 97.4 %all-to-all-start.1 = ((f32[128,8,1024]{2,1,0:T(8,128)}), f32[128,8,1024]{2,1,0:T(8,128)}, u32[]{:S(2)}, u32[]{:S(2)}) async-start(f32[128,8,1024]{2,1,0:T(8,128)} %fusion.2), calls=%async_computation.1 | async-start | bytes 8388608 | tf_op jit(solution)/shard_map/all_to_all | solution.py:13
where the time goes:
time: 250 us; the launch traced here: 249 us
  waiting for transfers between devices  116 us (46%)
  local copies, waits for them, and re-layouts  54.2 us (22%)
  matrix products  27.9 us (11%)
  other arithmetic  26.9 us (11%)
  starting transfers between devices  14.3 us (6%)
  blocking collectives  7.89 us (3%)
    all_to_all x1, waiting for transfers between devices, send_back(): lax.all_to_all(partial_value, 'blk', split_axis=0, concat_axis=1, tiled=T...  69.3 us
    all_to_all x1, waiting for transfers between devices, body(): lax.all_to_all(served, 'blk', split_axis=1, concat_axis=0, tiled=True)  46.9 us
    scatter-add x1, other arithmetic, body(): jnp.zeros(passages.shape, jnp.float32).at[:, requests, :].add(returned)  20.2 us
    gather x1, local copies, waits for them, and re-layouts, body(): jnp.take_along_axis(scores, target_slot[:, :, None], axis=2)[:, :, 0]  14.8 us
    dot_general x1, matrix products, body(): jnp.einsum('cpd,pk->ckd', contrib, merge_table, precision=lax.Precision.H...  13.3 us
    gather x2, local copies, waits for them, and re-layouts, body(): served = passages[:, requests, :]  11.6 us
    all_to_all x1, starting transfers between devices, body(): lax.all_to_all(served, 'blk', split_axis=1, concat_axis=0, tiled=True)  9.42 us
    unnamed x1, blocking collectives  7.89 us
  transfers between devices with their start and end apart: 2, of which 2 were waited for; matrix products, arithmetic and copies ran while one was open for 10% of the time, Pallas kernels for 0%

commit v1 on v0

--- a/solution.py
+++ b/solution.py
@@ -7,6 +7,27 @@
 BLK = 128
 NB = 4
 DISTINCT = 8
+
+
+def create_desk(local_array):
+    local_out = lax.axis_size("blk")
+    y_new = lax.axis_index("blk")
+    b_now, carry = (local_out, y_new)
+    s_next = local_array.shape[1] // b_now
+    finding = list(local_array.shape)
+    finding[1] = s_next
+    response = finding[0]
+    finding[0] = response * b_now
+    a_now = jnp.zeros(finding, local_array.dtype)
+    for no in range(b_now):
+        piece_next = lax.dynamic_slice_in_dim(local_array, (carry ^ no) * s_next, s_next, axis=1)
+        if no:
+            outer = range(b_now)
+            mat_out = map(lambda dev: (dev, dev ^ no), outer)
+            current_value = list(mat_out)
+            piece_next = lax.ppermute(piece_next, axis_name="blk", perm=current_value)
+        a_now = lax.dynamic_update_slice_in_dim(a_now, piece_next, (carry ^ no) * response, axis=0)
+    return a_now
 
 
 def send_back(partial_value):
@@ -29,7 +50,7 @@
     merge_table = matches.astype(jnp.float32)
     requests = lax.all_gather(jnp.maximum(wanted, 0), "blk", axis=0, tiled=True)
     served = passages[:, requests, :]
-    fetched = lax.all_to_all(served, "blk", split_axis=1, concat_axis=0, tiled=True)
+    fetched = create_desk(served)
     candidates = fetched[:, slot_index, :].reshape(BLK, qblocks_here, NB, D)
     query_rows = queries.reshape(qblocks_here, BLK, D)
     scores = jnp.einsum(

time: 250 us -> 283 us (1.13)
  starting transfers between devices: 14.3 us -> 36.8 us
  local copies, waits for them, and re-layouts: 54.2 us -> 66.6 us
  waiting for transfers between devices: 116 us -> 111 us
  other arithmetic: 26.9 us -> 30.8 us
    all_to_all x1 -> x0, waiting for transfers between devices: 46.9 us -> none  [body(): lax.all_to_all(served, 'blk', split_axis=1, concat_axis=0, tiled=True)]
    ppermute x0 -> x15, waiting for transfers between devices: none -> 41.5 us  [create_desk(): piece_next = lax.ppermute(piece_next, axis_name='blk', perm=current_value)]
    ppermute x0 -> x15, starting transfers between devices: none -> 28.6 us  [create_desk(): piece_next = lax.ppermute(piece_next, axis_name='blk', perm=current_value)]
    dynamic_update_slice x0 -> x16, local copies, waits for them, and re-layouts: none -> 16.2 us  [create_desk(): lax.dynamic_update_slice_in_dim(a_now, piece_next, (carry ^ no) * respons...]
    all_to_all x1 -> x0, starting transfers between devices: 9.42 us -> none  [body(): lax.all_to_all(served, 'blk', split_axis=1, concat_axis=0, tiled=True)]
    all_to_all x2 -> x0, local copies, waits for them, and re-layouts: 5.47 us -> none  [body(): lax.all_to_all(served, 'blk', split_axis=1, concat_axis=0, tiled=True)]
    gather x2 -> x1, local copies, waits for them, and re-layouts: 11.6 us -> 7.51 us  [body(): served = passages[:, requests, :]]
    all_to_all x1, starting transfers between devices: 4.91 us -> 8.25 us  [send_back(): lax.all_to_all(partial_value, 'blk', split_axis=0, concat_axis=1, tiled=T...]
  transfers between devices with their start and end apart: 2 -> 16, of which waited for: 2 -> 11; matrix products, arithmetic and copies ran while one was open for 10% -> 15% of each run, Pallas kernels for 0% -> 0%
where the time goes in v1:
time: 283 us; the launch traced here: 282 us
  waiting for transfers between devices  111 us (39%)
  local copies, waits for them, and re-layouts  66.6 us (24%)
  starting transfers between devices  36.8 us (13%)
  other arithmetic  30.8 us (11%)
  matrix products  27.7 us (10%)
  blocking collectives  7.89 us (3%)
    all_to_all x1, waiting for transfers between devices, send_back(): lax.all_to_all(partial_value, 'blk', split_axis=0, concat_axis=1, tiled=T...  69.3 us
    ppermute x15, waiting for transfers between devices, create_desk(): piece_next = lax.ppermute(piece_next, axis_name='blk', perm=current_value)  41.5 us
    ppermute x15, starting transfers between devices, create_desk(): piece_next = lax.ppermute(piece_next, axis_name='blk', perm=current_value)  28.6 us
    scatter-add x1, other arithmetic, body(): jnp.zeros(passages.shape, jnp.float32).at[:, requests, :].add(returned)  20.1 us
    dynamic_update_slice x16, local copies, waits for them, and re-layouts, create_desk(): lax.dynamic_update_slice_in_dim(a_now, piece_next, (carry ^ no) * respons...  16.2 us
    gather x1, local copies, waits for them, and re-layouts, body(): jnp.take_along_axis(scores, target_slot[:, :, None], axis=2)[:, :, 0]  14.8 us
    dot_general x1, matrix products, body(): jnp.einsum('cpd,pk->ckd', contrib, merge_table, precision=lax.Precision.H...  13.1 us
    all_to_all x1, starting transfers between devices, send_back(): lax.all_to_all(partial_value, 'blk', split_axis=0, concat_axis=1, tiled=T...  8.25 us
  transfers between devices with their start and end apart: 16, of which 11 were waited for; matrix products, arithmetic and copies ran while one was open for 15% of the time, Pallas kernels for 0%

profile of v1, /device:TPU:15, one launch (start us, length us, event | category | flops | bytes accessed | tf_op | source)
XLA Modules:
  0.0 282.2 jit_solution(856831358326870708)
XLA Ops:
  7.5 7.9 %all-reduce = s32[128]{0:T(128)S(1)} all-reduce(s32[128]{0:T(128)S(1)} %get-tuple-element.32), channel_id=1, replica_groups=mesh['groups'=2,'blk'=16] {'blk'}, use_global_device_ids=true, to_apply=%add | all-reduce | flops 128 | bytes 1024
  16.0 7.5 %gather_fusion = bf16[128,8,1024]{2,0,1:T(8,128)(2,1)} fusion(bf16[8,128,1024]{2,1,0:T(8,128)(2,1)} %param.6, s32[1024]{0:T(1024)S(1)} %pad_clamp_fusion.1), kind=kCustom, calls=%fused_computation | custom fusion | bytes 4194816 | tf_op jit(solution)/shard_map/gather | solution.py:52
  26.1 3.9 %collective-permute-start.14 = (bf16[8,8,1024]{2,1,0:T(8,128)(2,1)S(1)}, bf16[8,8,1024]{2,1,0:T(8,128)(2,1)}, u32[]{:S(2)}, u32[]{:S(2)}) collective-permute-start(bf16[8,8,1024]{2,1,0:T(8,128)(2,1)S(1)} %get-tuple-element.12), channel_id=1, source_target_pairs={{0,15},{1,14},{2,13},{3,12},{4,11},{5,10},{6,9},{7,8},{8,7},{9,6},... | collective-permute-start | bytes 393224 | tf_op jit(solution)/shard_map/ppermute | solution.py:28
  43.0 6.4 %collective-permute-done.1 = bf16[8,8,1024]{2,1,0:T(8,128)(2,1)S(1)} collective-permute-done((bf16[8,8,1024]{2,1,0:T(8,128)(2,1)S(1)}, bf16[8,8,1024]{2,1,0:T(8,128)(2,1)S(1)}, u32[]{:S(2)}, u32[]{:S(2)}) %collective-permute-start.1) | collective-permute-done | bytes 131104 | tf_op jit(solution)/shard_map/ppermute | solution.py:28
  51.2 4.3 %collective-permute-done.2 = bf16[8,8,1024]{2,1,0:T(8,128)(2,1)S(1)} collective-permute-done((bf16[8,8,1024]{2,1,0:T(8,128)(2,1)S(1)}, bf16[8,8,1024]{2,1,0:T(8,128)(2,1)S(1)}, u32[]{:S(2)}, u32[]{:S(2)}) %collective-permute-start.2) | collective-permute-done | bytes 131104 | tf_op jit(solution)/shard_map/ppermute | solution.py:28
  63.0 3.4 %collective-permute-done.4 = bf16[8,8,1024]{2,1,0:T(8,128)(2,1)S(1)} collective-permute-done((bf16[8,8,1024]{2,1,0:T(8,128)(2,1)S(1)}, bf16[8,8,1024]{2,1,0:T(8,128)(2,1)S(1)}, u32[]{:S(2)}, u32[]{:S(2)}) %collective-permute-start.4) | collective-permute-done | bytes 131104 | tf_op jit(solution)/shard_map/ppermute | solution.py:28
  67.9 3.9 %collective-permute-done.5 = bf16[8,8,1024]{2,1,0:T(8,128)(2,1)S(1)} collective-permute-done((bf16[8,8,1024]{2,1,0:T(8,128)(2,1)S(1)}, bf16[8,8,1024]{2,1,0:T(8,128)(2,1)S(1)}, u32[]{:S(2)}, u32[]{:S(2)}) %collective-permute-start.5) | collective-permute-done | bytes 131104 | tf_op jit(solution)/shard_map/ppermute | solution.py:28
  74.6 3.5 %collective-permute-done.6 = bf16[8,8,1024]{2,1,0:T(8,128)(2,1)S(1)} collective-permute-done((bf16[8,8,1024]{2,1,0:T(8,128)(2,1)S(1)}, bf16[8,8,1024]{2,1,0:T(8,128)(2,1)S(1)}, u32[]{:S(2)}, u32[]{:S(2)}) %collective-permute-start.6) | collective-permute-done | bytes 131104 | tf_op jit(solution)/shard_map/ppermute | solution.py:28
  80.1 5.2 %collective-permute-done.7 = bf16[8,8,1024]{2,1,0:T(8,128)(2,1)S(1)} collective-permute-done((bf16[8,8,1024]{2,1,0:T(8,128)(2,1)S(1)}, bf16[8,8,1024]{2,1,0:T(8,128)(2,1)S(1)}, u32[]{:S(2)}, u32[]{:S(2)}) %collective-permute-start.7) | collective-permute-done | bytes 131104 | tf_op jit(solution)/shard_map/ppermute | solution.py:28
  85.2 3.5 %collective-permute-start.8 = (bf16[8,8,1024]{2,1,0:T(8,128)(2,1)S(1)}, bf16[8,8,1024]{2,1,0:T(8,128)(2,1)S(1)}, u32[]{:S(2)}, u32[]{:S(2)}) collective-permute-start(bf16[8,8,1024]{2,1,0:T(8,128)(2,1)S(1)} %get-tuple-element.18), channel_id=1, source_target_pairs={{0,9},{1,8},{2,11},{3,10},{4,13},{5,12},{6,15},{7,14},{8,1},{9,0},... | collective-permute-start | bytes 393224 | tf_op jit(solution)/shard_map/ppermute | solution.py:28
  89.5 3.8 %collective-permute-done.8 = bf16[8,8,1024]{2,1,0:T(8,128)(2,1)S(1)} collective-permute-done((bf16[8,8,1024]{2,1,0:T(8,128)(2,1)S(1)}, bf16[8,8,1024]{2,1,0:T(8,128)(2,1)S(1)}, u32[]{:S(2)}, u32[]{:S(2)}) %collective-permute-start.8) | collective-permute-done | bytes 131104 | tf_op jit(solution)/shard_map/ppermute | solution.py:28
  93.2 3.9 %collective-permute-start.9 = (bf16[8,8,1024]{2,1,0:T(8,128)(2,1)S(1)}, bf16[8,8,1024]{2,1,0:T(8,128)(2,1)S(1)}, u32[]{:S(2)}, u32[]{:S(2)}) collective-permute-start(bf16[8,8,1024]{2,1,0:T(8,128)(2,1)S(1)} %get-tuple-element.17), channel_id=1, source_target_pairs={{0,10},{1,11},{2,8},{3,9},{4,14},{5,15},{6,12},{7,13},{8,2},{9,3},... | collective-permute-start | bytes 393224 | tf_op jit(solution)/shard_map/ppermute | solution.py:28
  97.9 4.2 %collective-permute-done.9 = bf16[8,8,1024]{2,1,0:T(8,128)(2,1)S(1)} collective-permute-done((bf16[8,8,1024]{2,1,0:T(8,128)(2,1)S(1)}, bf16[8,8,1024]{2,1,0:T(8,128)(2,1)S(1)}, u32[]{:S(2)}, u32[]{:S(2)}) %collective-permute-start.9) | collective-permute-done | bytes 131104 | tf_op jit(solution)/shard_map/ppermute | solution.py:28
  102.1 4.4 %collective-permute-start.10 = (bf16[8,8,1024]{2,1,0:T(8,128)(2,1)S(1)}, bf16[8,8,1024]{2,1,0:T(8,128)(2,1)S(1)}, u32[]{:S(2)}, u32[]{:S(2)}) collective-permute-start(bf16[8,8,1024]{2,1,0:T(8,128)(2,1)S(1)} %get-tuple-element.16), channel_id=1, source_target_pairs={{0,11},{1,10},{2,9},{3,8},{4,15},{5,14},{6,13},{7,12},{8,3},{9,2},... | collective-permute-start | bytes 393224 | tf_op jit(solution)/shard_map/ppermute | solution.py:28
  107.2 3.7 %collective-permute-done.10 = bf16[8,8,1024]{2,1,0:T(8,128)(2,1)S(1)} collective-permute-done((bf16[8,8,1024]{2,1,0:T(8,128)(2,1)S(1)}, bf16[8,8,1024]{2,1,0:T(8,128)(2,1)S(1)}, u32[]{:S(2)}, u32[]{:S(2)}) %collective-permute-start.10) | collective-permute-done | bytes 131104 | tf_op jit(solution)/shard_map/ppermute | solution.py:28
  118.2 6.8 %gather_fusion.1 = bf16[32,128,1024]{2,1,0:T(8,128)(2,1)} fusion(bf16[128,8,1024]{2,0,1:T(8,128)(2,1)} %copy_dynamic-update-slice_fusion, s32[1024]{0:T(1024)S(1)} %pad_clamp_fusion), kind=kCustom, calls=%fused_computation.1 | custom fusion | bytes 16777344 | tf_op jit(solution)/shard_map/gather | solution.py:54
  125.0 4.8 %fusion.5 = (f32[8,128]{1,0:T(8,128)S(1)}, f32[8,128,4,128]{3,1,2,0:T(8,128)S(1)}) fusion(pred[8,4,128]{2,1,0:T(4,128)(4,1)S(1)} %copy-done.6, bf16[128,8,4,1024]{3,0,2,1:T(8,128)(2,1)} %bitcast.112, bf16[8,128,1024,1]{2,1,3,0:T(8,128)(2,1)S(1)} %bitcast.107), kind=kOutput, calls=%fused_computation.11 | convolution fusion | flops 1074789376 | bytes 12591104 | tf_op jit(solution)/shard_map/grd,cgnd->grnc/dot_general | solution.py:56
  133.0 13.1 %fusion.2 = f32[128,8,1024]{2,1,0:T(8,128)} fusion(f32[128,32,1024]{2,0,1:T(8,128)S(1)} %bitcast.109, s32[32]{0:T(128)S(1)} %copy-done.17, s32[8]{0:T(128)S(1)} %copy-done.19), kind=kOutput, calls=%fused_computation.8 | convolution fusion | flops 402653440 | bytes 20971680 | tf_op jit(solution)/shard_map/cpd,pk->ckd/dot_general | solution.py:77
  146.1 8.3 %all-to-all-start = ((f32[128,8,1024]{2,1,0:T(8,128)}), f32[128,8,1024]{2,1,0:T(8,128)}, u32[]{:S(2)}, u32[]{:S(2)}) async-start(f32[128,8,1024]{2,1,0:T(8,128)} %fusion.2), calls=%async_computation | async-start | bytes 8388608 | tf_op jit(solution)/shard_map/all_to_all | solution.py:34
  154.7 14.8 %gather_fusion.2 = f32[1024]{0:T(1024)S(1)} fusion(f32[8,128,512]{1,2,0:T(8,128)} %bitcast.110, s32[1024]{0:T(1024)S(1)} %fusion.14), kind=kCustom, calls=%fused_computation.2 | custom fusion | bytes 20480 | tf_op jit(solution)/shard_map/jit(take_along_axis)/gather | solution.py:67
  170.2 7.3 %bitcast_convert_fusion = bf16[8,128,1024]{2,1,0:T(8,128)(2,1)} fusion(bf16[128,8,4,1024]{3,0,2,1:T(8,128)(2,1)} %bitcast.113, f32[8,128,4,128]{3,1,2,0:T(8,128)} %copy-done.1, s32[8,128]{1,0:T(8,128)S(1)} %add_select_fusion, s32[4,128]{1,0:T(4,128)S(1)} %copy-done.9, f32[8,128]{1,0:T(8,128)S(1)} %fusion.8, f32[8,128]{1,0:T(8,128)S(1)} %get-tuple-element.30, ...), kind=kOutput, calls=%fused_computation.7 | convolution fusion | flops 1078460416 | bytes 12601344 | tf_op jit(solution)/shard_map/grnc,cgnd->grd/dot_general | solution.py:78
  177.6 69.3 %all-to-all-done = f32[128,8,1024]{2,1,0:T(8,128)} async-done(((f32[128,8,1024]{2,1,0:T(8,128)}), f32[128,8,1024]{2,1,0:T(8,128)}, u32[]{:S(2)}, u32[]{:S(2)}) %all-to-all-start) | async-done | bytes 4194336 | tf_op jit(solution)/shard_map/all_to_all | solution.py:34
  246.9 7.7 %copy.40 = f32[8,16,8,1024]{3,0,2,1:T(8,128)} copy(f32[8,16,8,1024]{3,2,0,1:T(8,128)} %bitcast.44) | data formatting | bytes 8388608 | tf_op jit(solution)/shard_map/all_to_all | solution.py:34
  257.1 20.1 %scatter_fusion = f32[8,128,1024]{2,0,1:T(8,128)} fusion(f32[8,128,1024]{2,0,1:T(8,128)} %broadcast_in_dim.54, s32[128]{0:T(128)S(1)} %copy-done.15, f32[128,8,1024]{2,1,0:T(8,128)} %bitcast.111), kind=kCustom, calls=%fused_computation.4 | custom fusion | flops 1048576 | bytes 12583424 | tf_op jit(solution)/shard_map/scatter-add | solution.py:82
  (112 shorter events, 58.9 us)
Async XLA Ops:
  0.6 124.4 %copy-start = (bf16[1024,1024]{1,0:T(8,128)(2,1)S(1)}, bf16[1024,1024]{1,0:T(8,128)(2,1)}, u32[]{:S(2)}) copy-start(bf16[1024,1024]{1,0:T(8,128)(2,1)} %param.5) | copy-start | bytes 6291460
  1.7 33.2 %copy-start.16 = (s32[32]{0:T(128)}, s32[32]{0:T(128)S(1)}, u32[]{:S(2)}) copy-start(s32[32]{0:T(128)S(1)} %reshape.340) | copy-start | bytes 388
  6.3 28.6 %copy-start.18 = (s32[8]{0:T(128)}, s32[8]{0:T(128)S(1)}, u32[]{:S(2)}) copy-start(s32[8]{0:T(128)S(1)} %scatter_custom_fusion) | copy-start | bytes 100
  23.5 10.3 %copy-start.20 = (s32[8]{0:T(128)S(1)}, s32[8]{0:T(128)}, u32[]{:S(2)}) copy-start(s32[8]{0:T(128)} %param.8) | copy-start | bytes 100
  26.1 90.5 %collective-permute-start.14 = (bf16[8,8,1024]{2,1,0:T(8,128)(2,1)S(1)}, bf16[8,8,1024]{2,1,0:T(8,128)(2,1)}, u32[]{:S(2)}, u32[]{:S(2)}) collective-permute-start(bf16[8,8,1024]{2,1,0:T(8,128)(2,1)S(1)} %get-tuple-element.12), channel_id=1, source_target_pairs={{0,15},{1,14},{2,13},{3,12},{4,11},{5,10},{6,9},{7,8},{8,7},{9,6},... | collective-permute-start | bytes 393224 | tf_op jit(solution)/shard_map/ppermute | solution.py:28
  30.1 84.9 %collective-permute-start.13 = (bf16[8,8,1024]{2,1,0:T(8,128)(2,1)S(1)}, bf16[8,8,1024]{2,1,0:T(8,128)(2,1)}, u32[]{:S(2)}, u32[]{:S(2)}) collective-permute-start(bf16[8,8,1024]{2,1,0:T(8,128)(2,1)S(1)} %get-tuple-element.13), channel_id=1, source_target_pairs={{0,14},{1,15},{2,12},{3,13},{4,10},{5,11},{6,8},{7,9},{8,6},{9,7},... | collective-permute-start | bytes 393224 | tf_op jit(solution)/shard_map/ppermute | solution.py:28
  31.7 81.7 %collective-permute-start.12 = (bf16[8,8,1024]{2,1,0:T(8,128)(2,1)S(1)}, bf16[8,8,1024]{2,1,0:T(8,128)(2,1)}, u32[]{:S(2)}, u32[]{:S(2)}) collective-permute-start(bf16[8,8,1024]{2,1,0:T(8,128)(2,1)S(1)} %get-tuple-element.14), channel_id=1, source_target_pairs={{0,13},{1,12},{2,15},{3,14},{4,9},{5,8},{6,11},{7,10},{8,5},{9,4},... | collective-permute-start | bytes 393224 | tf_op jit(solution)/shard_map/ppermute | solution.py:28
  31.7 79.9 %collective-permute-start.11 = (bf16[8,8,1024]{2,1,0:T(8,128)(2,1)S(1)}, bf16[8,8,1024]{2,1,0:T(8,128)(2,1)}, u32[]{:S(2)}, u32[]{:S(2)}) collective-permute-start(bf16[8,8,1024]{2,1,0:T(8,128)(2,1)S(1)} %get-tuple-element.15), channel_id=1, source_target_pairs={{0,12},{1,13},{2,14},{3,15},{4,8},{5,9},{6,10},{7,11},{8,4},{9,5},... | collective-permute-start | bytes 393224 | tf_op jit(solution)/shard_map/ppermute | solution.py:28
  31.9 8.4 %collective-permute-start = (bf16[8,8,1024]{2,1,0:T(8,128)(2,1)}, bf16[8,8,1024]{2,1,0:T(8,128)(2,1)}, u32[]{:S(2)}, u32[]{:S(2)}) collective-permute-start(bf16[8,8,1024]{2,1,0:T(8,128)(2,1)} %get-tuple-element.26), channel_id=1, source_target_pairs={{0,1},{1,0},{2,3},{3,2},{4,5},{5,4},{6,7},{7,6},{8,9},{9,8},{10,11... | collective-permute-start | bytes 393224 | tf_op jit(solution)/shard_map/ppermute | solution.py:28
  36.3 13.1 %copy-start.4 = (bf16[8,8,1024]{2,1,0:T(8,128)(2,1)S(1)}, bf16[8,8,1024]{2,1,0:T(8,128)(2,1)}, u32[]{:S(2)}) copy-start(bf16[8,8,1024]{2,1,0:T(8,128)(2,1)} %get-tuple-element.24) | copy-start | bytes 393220
  36.3 19.2 %copy-start.3 = (bf16[8,8,1024]{2,1,0:T(8,128)(2,1)S(1)}, bf16[8,8,1024]{2,1,0:T(8,128)(2,1)}, u32[]{:S(2)}) copy-start(bf16[8,8,1024]{2,1,0:T(8,128)(2,1)} %get-tuple-element.23) | copy-start | bytes 393220
  36.3 23.9 %copy-start.2 = (bf16[8,8,1024]{2,1,0:T(8,128)(2,1)S(1)}, bf16[8,8,1024]{2,1,0:T(8,128)(2,1)}, u32[]{:S(2)}) copy-start(bf16[8,8,1024]{2,1,0:T(8,128)(2,1)} %get-tuple-element.22) | copy-start | bytes 393220
  40.4 9.0 %collective-permute-start.1 = (bf16[8,8,1024]{2,1,0:T(8,128)(2,1)S(1)}, bf16[8,8,1024]{2,1,0:T(8,128)(2,1)S(1)}, u32[]{:S(2)}, u32[]{:S(2)}) collective-permute-start(bf16[8,8,1024]{2,1,0:T(8,128)(2,1)S(1)} %copy-done.5), channel_id=1, source_target_pairs={{0,2},{1,3},{2,0},{3,1},{4,6},{5,7},{6,4},{7,5},{8,10},{9,11},{10,... | collective-permute-start | bytes 393224 | tf_op jit(solution)/shard_map/ppermute | solution.py:28
  49.4 6.1 %collective-permute-start.2 = (bf16[8,8,1024]{2,1,0:T(8,128)(2,1)S(1)}, bf16[8,8,1024]{2,1,0:T(8,128)(2,1)S(1)}, u32[]{:S(2)}, u32[]{:S(2)}) collective-permute-start(bf16[8,8,1024]{2,1,0:T(8,128)(2,1)S(1)} %copy-done.4), channel_id=1, source_target_pairs={{0,3},{1,2},{2,1},{3,0},{4,7},{5,6},{6,5},{7,4},{8,11},{9,10},{10,... | collective-permute-start | bytes 393224 | tf_op jit(solution)/shard_map/ppermute | solution.py:28
  55.5 4.7 %collective-permute-start.3 = (bf16[8,8,1024]{2,1,0:T(8,128)(2,1)S(1)}, bf16[8,8,1024]{2,1,0:T(8,128)(2,1)S(1)}, u32[]{:S(2)}, u32[]{:S(2)}) collective-permute-start(bf16[8,8,1024]{2,1,0:T(8,128)(2,1)S(1)} %copy-done.3), channel_id=1, source_target_pairs={{0,4},{1,5},{2,6},{3,7},{4,0},{5,1},{6,2},{7,3},{8,12},{9,13},{10,... | collective-permute-start | bytes 393224 | tf_op jit(solution)/shard_map/ppermute | solution.py:28
  60.2 6.3 %collective-permute-start.4 = (bf16[8,8,1024]{2,1,0:T(8,128)(2,1)S(1)}, bf16[8,8,1024]{2,1,0:T(8,128)(2,1)S(1)}, u32[]{:S(2)}, u32[]{:S(2)}) collective-permute-start(bf16[8,8,1024]{2,1,0:T(8,128)(2,1)S(1)} %copy-done.2), channel_id=1, source_target_pairs={{0,5},{1,4},{2,7},{3,6},{4,1},{5,0},{6,3},{7,2},{8,13},{9,12},{10,... | collective-permute-start | bytes 393224 | tf_op jit(solution)/shard_map/ppermute | solution.py:28
  66.4 5.4 %collective-permute-start.5 = (bf16[8,8,1024]{2,1,0:T(8,128)(2,1)S(1)}, bf16[8,8,1024]{2,1,0:T(8,128)(2,1)S(1)}, u32[]{:S(2)}, u32[]{:S(2)}) collective-permute-start(bf16[8,8,1024]{2,1,0:T(8,128)(2,1)S(1)} %get-tuple-element.21), channel_id=1, source_target_pairs={{0,6},{1,7},{2,4},{3,5},{4,2},{5,3},{6,0},{7,1},{8,14},{9,15},{10,... | collective-permute-start | bytes 393224 | tf_op jit(solution)/shard_map/ppermute | solution.py:28
  71.8 6.3 %collective-permute-start.6 = (bf16[8,8,1024]{2,1,0:T(8,128)(2,1)S(1)}, bf16[8,8,1024]{2,1,0:T(8,128)(2,1)S(1)}, u32[]{:S(2)}, u32[]{:S(2)}) collective-permute-start(bf16[8,8,1024]{2,1,0:T(8,128)(2,1)S(1)} %get-tuple-element.20), channel_id=1, source_target_pairs={{0,7},{1,6},{2,5},{3,4},{4,3},{5,2},{6,1},{7,0},{8,15},{9,14},{10,... | collective-permute-start | bytes 393224 | tf_op jit(solution)/shard_map/ppermute | solution.py:28
  78.1 7.2 %collective-permute-start.7 = (bf16[8,8,1024]{2,1,0:T(8,128)(2,1)S(1)}, bf16[8,8,1024]{2,1,0:T(8,128)(2,1)S(1)}, u32[]{:S(2)}, u32[]{:S(2)}) collective-permute-start(bf16[8,8,1024]{2,1,0:T(8,128)(2,1)S(1)} %get-tuple-element.19), channel_id=1, source_target_pairs={{0,8},{1,9},{2,10},{3,11},{4,12},{5,13},{6,14},{7,15},{8,0},{9,1},... | collective-permute-start | bytes 393224 | tf_op jit(solution)/shard_map/ppermute | solution.py:28
  85.2 8.0 %collective-permute-start.8 = (bf16[8,8,1024]{2,1,0:T(8,128)(2,1)S(1)}, bf16[8,8,1024]{2,1,0:T(8,128)(2,1)S(1)}, u32[]{:S(2)}, u32[]{:S(2)}) collective-permute-start(bf16[8,8,1024]{2,1,0:T(8,128)(2,1)S(1)} %get-tuple-element.18), channel_id=1, source_target_pairs={{0,9},{1,8},{2,11},{3,10},{4,13},{5,12},{6,15},{7,14},{8,1},{9,0},... | collective-permute-start | bytes 393224 | tf_op jit(solution)/shard_map/ppermute | solution.py:28
  93.2 8.9 %collective-permute-start.9 = (bf16[8,8,1024]{2,1,0:T(8,128)(2,1)S(1)}, bf16[8,8,1024]{2,1,0:T(8,128)(2,1)S(1)}, u32[]{:S(2)}, u32[]{:S(2)}) collective-permute-start(bf16[8,8,1024]{2,1,0:T(8,128)(2,1)S(1)} %get-tuple-element.17), channel_id=1, source_target_pairs={{0,10},{1,11},{2,8},{3,9},{4,14},{5,15},{6,12},{7,13},{8,2},{9,3},... | collective-permute-start | bytes 393224 | tf_op jit(solution)/shard_map/ppermute | solution.py:28
  102.1 8.8 %collective-permute-start.10 = (bf16[8,8,1024]{2,1,0:T(8,128)(2,1)S(1)}, bf16[8,8,1024]{2,1,0:T(8,128)(2,1)S(1)}, u32[]{:S(2)}, u32[]{:S(2)}) collective-permute-start(bf16[8,8,1024]{2,1,0:T(8,128)(2,1)S(1)} %get-tuple-element.16), channel_id=1, source_target_pairs={{0,11},{1,10},{2,9},{3,8},{4,15},{5,14},{6,13},{7,12},{8,3},{9,2},... | collective-permute-start | bytes 393224 | tf_op jit(solution)/shard_map/ppermute | solution.py:28
  146.1 8.3 %copy-start.13 = (pred[8]{0:T(512)(128)(4,1)S(1)}, pred[8]{0:T(512)(128)(4,1)}, u32[]{:S(2)}) copy-start(pred[8]{0:T(512)(128)(4,1)} %broadcast_compare_fusion.1) | copy-start | bytes 28
  146.1 100.7 %all-to-all-start = ((f32[128,8,1024]{2,1,0:T(8,128)}), f32[128,8,1024]{2,1,0:T(8,128)}, u32[]{:S(2)}, u32[]{:S(2)}) async-start(f32[128,8,1024]{2,1,0:T(8,128)} %fusion.2), calls=%async_computation | async-start | bytes 8388608 | tf_op jit(solution)/shard_map/all_to_all | solution.py:34
  (13 other events, 50.8 us)
